TPU v7x, 128 devices: a whole 4x4x4 slice. The times are simulated.
128 devices in a mesh: wide: 16 (over y, z), grp: 8 (over x, core).
Axes of the slice: x: 4, y: 4, z: 4, core: 2. Of those that a mesh axis runs over, the one named last changes fastest.
Arguments:
- eta_hat: bfloat16 [2, 2048, 2048], P(None, ('wide', 'grp')), may hold values from -0.0008544922 to 0.0008544922
- phi_hat: bfloat16 [2, 2048, 2048], P(None, ('wide', 'grp')), may hold values from -0.00061035156 to 0.00061035156
- patch_tiles: int32 [256], replicated, may hold values from 0 to 1023, as said below
- fraction: bfloat16 [2, 128, 64, 128, 128], P(None, ('wide', 'grp')), may hold values from 0 to 1
Outputs:
- surface: float32 [2048, 2048], P(('wide', 'grp'))
- fraction_next: bfloat16 [2, 128, 64, 128, 128], P(None, ('wide', 'grp'))
- tendency: float32 [2, 2048, 2048], P(None, ('wide', 'grp'))
Inputs may be any that keep to these rules, and one draw needn't show every extreme that they name: `patch_tiles`: for each g below 8, entries g * 32 to (g + 1) * 32 - 1 are distinct tiles, in ascending order, whose column t % 32 lies in [g * 4, (g + 1) * 4). Of these, the tiles of one band (rows (t // 32) // 2 equal) are at most 8, and in every group one band holds exactly 8.
All inputs are finite; a program needn't handle non-finite values.
Results may differ from a plain program's by a relative error of at most 0.019.
Values may be sent and summed in bfloat16 or wider, within the bound.
A program may use at most 192 MiB of HBM per device.

v0:
```python
import math
import jax
import jax.numpy as jnp
from jax import lax
from jax.sharding import PartitionSpec as P

RADIX = 32
TS = 64
Z_BOTTOM = -2.0
Z_TOP = 2.0
DECAY_RATE = 0.5
COURANT = 0.3


def for_sending(shard):

    def short(part):
        return part.astype(jnp.bfloat16) if part.dtype == jnp.float32 else part

    return jax.tree.map(short, shard)


def refine(field):
    return jnp.repeat(jnp.repeat(field, 2, axis=0), 2, axis=1)


def upwind_flux(values, speeds, axis):
    widths = tuple(((1, 1) if dim_index == axis else (0, 0) for dim_index in range(3)))
    padded = jnp.pad(values, widths, mode="edge")
    speed_pad = jnp.pad(speeds, widths, mode="edge")
    count_faces = padded.shape[axis] - 1
    left_vals = lax.slice_in_dim(padded, 0, count_faces, axis=axis)
    right_vals = lax.slice_in_dim(padded, 1, count_faces + 1, axis=axis)
    face_speed = 0.5 * (
        lax.slice_in_dim(speed_pad, 0, count_faces, axis=axis)
        + lax.slice_in_dim(speed_pad, 1, count_faces + 1, axis=axis)
    )
    face_flux = jnp.maximum(face_speed, 0.0) * left_vals + jnp.minimum(face_speed, 0.0) * right_vals
    return lax.slice_in_dim(face_flux, 1, count_faces, axis=axis) - lax.slice_in_dim(
        face_flux, 0, count_faces - 1, axis=axis
    )


def patch_step(state, height, along_x, along_y):
    levels = state.shape[0]
    side = state.shape[1]
    spacing = (Z_TOP - Z_BOTTOM) / levels
    level_z = (Z_BOTTOM + (jnp.arange(levels, dtype=jnp.float32) + 0.5) * spacing)[:, None, None]
    fine_h = refine(height)[None]
    from_sea = jnp.clip((fine_h - level_z) / spacing + 0.5, 0.0, 1.0)
    position = jnp.arange(side, dtype=jnp.float32)
    edge_dist = jnp.minimum(position, side - 1.0 - position)
    distance = jnp.minimum(edge_dist[:, None], edge_dist[None, :])
    weight = 0.3 + 0.7 * jnp.exp(-8.0 * distance / side)
    blended = weight * from_sea + (1.0 - weight) * state.astype(jnp.float32)
    profile = jnp.exp(DECAY_RATE * (level_z - Z_TOP))
    speed_x = refine(along_x)[None] * profile
    speed_y = refine(along_y)[None] * profile
    moved = blended - COURANT * (
        upwind_flux(blended, speed_x, 2) + upwind_flux(blended, speed_y, 1)
    )
    updated = jnp.clip(moved, 0.0, 1.0)
    column = Z_BOTTOM + spacing * jnp.sum(updated, axis=0)
    coarse = column.reshape(side // 2, 2, side // 2, 2).mean(axis=(1, 3))
    return (updated.astype(jnp.bfloat16), coarse)


def small_tables(length):
    index_row = jnp.arange(length, dtype=jnp.int32)
    phase = index_row[:, None] * index_row[None, :] % length
    angle = phase.astype(jnp.float32) * (2.0 * math.pi / length)
    return (jnp.cos(angle).astype(jnp.bfloat16), jnp.sin(angle).astype(jnp.bfloat16))


def contract(data, table, pattern):
    return jnp.einsum(pattern, data, table, preferred_element_type=jnp.float32)


def factored_transform(real_in, imag_in, direction_sign, real_only):
    length = real_in.shape[-1]
    leading = real_in.shape[:-1]
    inner_size = length // RADIX
    cos_p, sin_p = small_tables(RADIX)
    cos_q, sin_q = small_tables(inner_size)
    split_re = real_in.reshape(leading + (RADIX, inner_size))
    segment_re = contract(split_re, cos_p, "...pq,pk->...kq")
    segment_im = direction_sign * contract(split_re, sin_p, "...pq,pk->...kq")
    if imag_in is not None:
        split_im = imag_in.reshape(leading + (RADIX, inner_size))
        segment_re = segment_re - direction_sign * contract(split_im, sin_p, "...pq,pk->...kq")
        segment_im = segment_im + contract(split_im, cos_p, "...pq,pk->...kq")
    first_idx = jnp.arange(RADIX, dtype=jnp.int32)[:, None]
    second_idx = jnp.arange(inner_size, dtype=jnp.int32)[None, :]
    angle = (first_idx * second_idx % length).astype(jnp.float32) * (2.0 * math.pi / length)
    twist_cos = jnp.cos(angle)
    twist_sin = jnp.sin(angle)
    turned_re = (segment_re * twist_cos - direction_sign * segment_im * twist_sin).astype(
        jnp.bfloat16
    )
    turned_im = (segment_im * twist_cos + direction_sign * segment_re * twist_sin).astype(
        jnp.bfloat16
    )
    out_re = contract(turned_re, cos_q, "...kq,qm->...km") - direction_sign * contract(
        turned_im, sin_q, "...kq,qm->...km"
    )
    out_re = jnp.swapaxes(out_re, -1, -2).reshape(leading + (length,))
    if real_only:
        return out_re
    out_im = contract(turned_im, cos_q, "...kq,qm->...km") + direction_sign * contract(
        turned_re, sin_q, "...kq,qm->...km"
    )
    out_im = jnp.swapaxes(out_im, -1, -2).reshape(leading + (length,))
    return (out_re, out_im)


def signed_waves(index_values, length):
    signed = (index_values + length // 2) % length - length // 2
    return signed.astype(jnp.float32) * (2.0 * math.pi / length)


def shards(eta_hat, phi_hat, patch_tiles, fraction):
    row_count = eta_hat.shape[1]
    length = eta_hat.shape[2]
    n_wide = lax.axis_size("wide")
    me_wide = lax.axis_index("wide")
    me_grp = lax.axis_index("grp")
    me_flat = lax.axis_index(("wide", "grp"))
    wave_cols = signed_waves(jnp.arange(length, dtype=jnp.int32), length)
    wave_rows = signed_waves(me_flat * row_count + jnp.arange(row_count, dtype=jnp.int32), length)
    phi_re = phi_hat[0].astype(jnp.float32)
    phi_im = phi_hat[1].astype(jnp.float32)
    real_in = jnp.stack(
        [
            eta_hat[0],
            (-wave_rows[:, None] * phi_im).astype(jnp.bfloat16),
            (-wave_cols[None, :] * phi_im).astype(jnp.bfloat16),
        ]
    )
    imag_in = jnp.stack(
        [
            eta_hat[1],
            (wave_rows[:, None] * phi_re).astype(jnp.bfloat16),
            (wave_cols[None, :] * phi_re).astype(jnp.bfloat16),
        ]
    )
    half_re, half_im = factored_transform(real_in, imag_in, 1.0, False)
    inverse_rows = jnp.swapaxes(
        jnp.concatenate([half_re.astype(jnp.bfloat16), half_im.astype(jnp.bfloat16)]), 1, 2
    )
    turned = lax.all_to_all(inverse_rows, ("wide", "grp"), split_axis=1, concat_axis=2, tiled=True)
    physical = factored_transform(turned[0:3], turned[3:6], 1.0, True)
    band_fields = lax.all_to_all(
        physical.astype(jnp.bfloat16), "grp", split_axis=2, concat_axis=1, tiled=True
    ).astype(physical.dtype)
    band_rows = band_fields.shape[1]
    band_cols = band_fields.shape[2]
    tile_rows = band_rows // TS
    tile_cols = band_cols // TS
    tiles_side = length // TS
    per_group = 2 * n_wide
    group_list = lax.dynamic_slice_in_dim(patch_tiles, me_grp * per_group, per_group)
    row_of = group_list // tiles_side
    col_of = group_list % tiles_side - me_grp * tile_cols
    my_ranks = jnp.arange(2, dtype=jnp.int32) * n_wide + me_wide
    local_t = jnp.arange(tile_rows * tile_cols, dtype=jnp.int32)
    tile_id = (
        (me_wide * tile_rows + local_t // tile_cols) * tiles_side
        + me_grp * tile_cols
        + local_t % tile_cols
    )
    matches = tile_id[:, None] == group_list[None, :]
    active = jnp.any(matches, axis=1)
    rank_index = jnp.sum(
        jnp.where(matches, jnp.arange(per_group, dtype=jnp.int32)[None, :], 0), axis=1
    )
    column_strip = lax.all_gather(
        band_fields.astype(jnp.bfloat16), "wide", axis=1, tiled=True
    ).astype(band_fields.dtype)

    def pick_strip(rank):
        return lax.dynamic_slice(
            column_strip, (0, row_of[rank] * TS, col_of[rank] * TS), (3, TS, TS)
        )

    footprints = jax.vmap(pick_strip)(my_ranks)
    new_states, coarse = jax.vmap(patch_step)(
        fraction[:, 0], footprints[:, 0], footprints[:, 1], footprints[:, 2]
    )
    coarse_flat = coarse.reshape(2, TS * TS)
    every_result = (
        lax.all_gather(
            coarse_flat.reshape(2, 1, TS * TS).astype(jnp.bfloat16), "wide", axis=1, tiled=True
        )
        .astype(jnp.float32)
        .reshape(per_group, TS * TS)
    )
    picked = every_result[rank_index]
    band_tiles = (
        band_fields[0]
        .reshape(tile_rows, TS, tile_cols, TS)
        .transpose(0, 2, 1, 3)
        .reshape(tile_rows * tile_cols, TS * TS)
    )
    corrected = jnp.where(active[:, None], picked, band_tiles)
    surface_band = (
        corrected.reshape(tile_rows, tile_cols, TS, TS)
        .transpose(0, 2, 1, 3)
        .reshape(band_rows, band_cols)
    )
    surface = lax.all_to_all(
        for_sending(surface_band), "grp", split_axis=0, concat_axis=1, tiled=True
    ).astype(surface_band.dtype)
    along_x = physical[1]
    along_y = physical[2]
    drive = (-(surface + 0.5 * (along_x * along_x + along_y * along_y))).astype(jnp.bfloat16)
    drive_re, drive_im = factored_transform(drive, None, -1.0, False)
    pair_rows = jnp.swapaxes(
        jnp.stack([drive_re.astype(jnp.bfloat16), drive_im.astype(jnp.bfloat16)]), 1, 2
    )
    pair_cols = lax.all_to_all(pair_rows, ("wide", "grp"), split_axis=1, concat_axis=2, tiled=True)
    spec_re, spec_im = factored_transform(pair_cols[0], pair_cols[1], -1.0, False)
    tendency = jnp.stack([spec_re, spec_im]) * (1.0 / length)
    return (surface, new_states[:, None], tendency)


def solution(mesh):
    placed = (
        P(None, ("wide", "grp"), None),
        P(None, ("wide", "grp"), None),
        P(),
        P(None, ("wide", "grp"), None, None, None),
    )
    return jax.shard_map(
        shards,
        mesh=mesh,
        in_specs=placed,
        out_specs=(
            P(("wide", "grp"), None),
            P(None, ("wide", "grp"), None, None, None),
            P(None, ("wide", "grp"), None),
        ),
        check_vma=False,
    )
```

profile of v0, /device:TPU:1, one launch (start us, length us, event | category | flops | bytes accessed | tf_op | source)
XLA Modules:
  0.0 338.8 jit_solution(14497222716978649175)
XLA Ops:
  15.9 4.1 %copy.124 = bf16[6,2048,16]{2,0,1:T(8,128)(2,1)} copy(bf16[6,2048,16]{1,2,0:T(8,128)(2,1)S(1)} %maximum_bitcast_fusion) | data formatting | bytes 786432 | tf_op jit(solution)/shard_map/transpose | solution.py:147
  20.0 5.6 %reshape.527 = bf16[128,2,768]{2,1,0:T(2,128)(2,1)S(1)} reshape(bf16[2048,6,16]{2,1,0:T(8,128)(2,1)} %bitcast.240) | data formatting | bytes 786432
  25.6 24.1 %all_to_all.58 = bf16[128,2,768]{2,1,0:T(2,128)(2,1)S(1)} all-to-all(bf16[128,2,768]{2,1,0:T(2,128)(2,1)S(1)} %reshape.527), channel_id=1, replica_groups=mesh['wide'=16,'grp'=8] {'wide','grp'}, dimensions={0} | all-to-all | bytes 786432 | tf_op jit(solution)/shard_map/all_to_all | solution.py:150
  49.7 4.8 %reshape.528 = bf16[2048,6,16]{2,1,0:T(8,128)(2,1)} reshape(bf16[128,2,768]{2,1,0:T(2,128)(2,1)S(1)} %all_to_all.58) | data formatting | bytes 786432
  54.6 6.1 %copy.158 = bf16[6,128,16,16]{2,1,3,0:T(8,128)(2,1)S(1)} copy(bf16[6,128,16,16]{3,0,2,1:T(8,128)(2,1)} %bitcast.239) | data formatting | bytes 786432 | tf_op jit(solution)/shard_map/all_to_all | solution.py:150
  62.6 4.3 %copy.126 = bf16[3,16,128,16]{3,2,1,0:T(8,128)(2,1)S(1)} copy(bf16[3,16,128,16]{1,2,3,0:T(8,128)(2,1)} %get-tuple-element.58) | data formatting | bytes 393216 | tf_op jit(solution)/shard_map/slice | solution.py:151
  70.2 3.1 copy.127
  77.9 3.4 %copy.159 = bf16[3,16,64,32]{1,0,3,2:T(4,128)(2,1)S(1)} copy(bf16[3,16,64,32]{2,3,1,0:T(8,128)(2,1)S(1)} %get-tuple-element.82) | data formatting | bytes 393216 | tf_op jit(solution)/shard_map/convert_element_type | solution.py:153
  83.2 9.3 %all_to_all.59 = bf16[8,2,6144]{2,1,0:T(2,128)(2,1)S(1)} all-to-all(bf16[8,2,6144]{2,1,0:T(2,128)(2,1)S(1)} %reshape.529), channel_id=1, replica_groups=mesh['wide'=16,'grp'=8] {'grp'}, dimensions={0} | all-to-all | bytes 393216 | tf_op jit(solution)/shard_map/all_to_all | solution.py:152
  94.5 2.0 copy.161
  101.1 39.6 %all-gather.2.cloned.1.call-done = bf16[3,2048,256]{2,1,0:T(8,128)(2,1)} async-done(((bf16[3,128,256]{2,1,0:T(8,128)(2,1)}), bf16[3,2048,256]{2,1,0:T(8,128)(2,1)}) %all-gather.2.cloned.1.call-update) | async-done | bytes 3145744 | tf_op jit(solution)/shard_map/all_gather | solution.py:176
  140.7 5.1 %convert_element_type.418 = f32[3,2048,256]{2,1,0:T(8,128)} convert(bf16[3,2048,256]{2,1,0:T(8,128)(2,1)} %all-gather.2.cloned.1.call-done) | non-fusion elementwise | flops 1572864 | bytes 9437184 | tf_op jit(solution)/shard_map/convert_element_type | solution.py:178
  145.8 5.9 %while.1 = (s32[]{:T(128)}, f32[3,2048,256]{2,1,0:T(8,128)}, s32[2,3]{1,0:T(2,128)S(1)}, f32[2,3,64,64]{3,2,1,0:T(8,128)S(1)}, s32[]{:T(128)}) while((s32[]{:T(128)}, f32[3,2048,256]{2,1,0:T(8,128)}, s32[2,3]{1,0:T(2,128)S(1)}, f32[2,3,64,64]{3,2,1,0:T(8,128)S(1)}, s32[]{:T(128)}) %tuple.55), condition=%wide.while_cond, body=%wide.while_body.sunk | while | flops 2 | bytes 147581 | solution.py:181
  146.4 2.3 bitcast_dynamic-update-slice_fusion.2
  149.3 2.3 bitcast_dynamic-update-slice_fusion.2
  153.6 3.9 %fusion.8 = f32[2,64,128,128]{3,2,1,0:T(8,128)S(1)} fusion(bf16[2,1,64,128,128]{4,3,2,1,0:T(8,128)(2,1)} %param.7, f32[128,128]{1,0:T(8,128)S(1)} %get-tuple-element.81, f32[64]{0:T(128)S(1)} %fusion.129, f32[2,128,128]{2,1,0:T(8,128)S(1)} %copy.134, f32[128,128]{1,0:T(8,128)S(1)} %get-tuple-element.80), kind=kLoop, calls=%fused_computation.22 | loop fusion | flops 16777216 | bytes 12845312 | tf_op jit(solution)/shard_map/vmap()/add | solution.py:55
  157.6 7.7 %fusion.246 = (f32[2,64,128,1]{3,2,1,0:T(8,128)}, f32[2,64,128,1]{3,2,1,0:T(8,128)}) fusion(f32[2,64,128,128]{3,2,1,0:T(8,128)S(1)} %fusion.8), kind=kLoop, calls=%fused_computation.353 | loop fusion | bytes 262144 | tf_op jit(solution)/shard_map/vmap(jit(_pad))/slice | solution.py:29
  166.5 5.4 %broadcast_multiply_fusion.1 = (f32[2,64,128,128]{3,2,1,0:T(8,128)}, f32[2,64,128,128]{3,2,1,0:T(8,128)S(1)}) fusion(f32[64]{0:T(128)S(1)} %multiply_exponential_fusion, f32[2,128,128]{2,1,0:T(8,128)S(1)} %copy.137, f32[2,128,128]{2,1,0:T(8,128)S(1)} %copy.139), kind=kLoop, calls=%fused_computation.25 | loop fusion | flops 4194304 | bytes 17039616 | tf_op jit(solution)/shard_map/vmap()/mul | solution.py:57
  171.9 3.2 copy-done.1
  175.2 13.3 %fusion.245 = (f32[2,64,128,1]{3,2,1,0:T(8,128)}, f32[2,64,128,1]{3,2,1,0:T(8,128)}) fusion(f32[2,64,128,128]{3,2,1,0:T(8,128)} %get-tuple-element.78), kind=kLoop, calls=%fused_computation.352 | loop fusion | bytes 262144 | tf_op jit(solution)/shard_map/vmap(jit(_pad))/slice | solution.py:30
  188.5 12.6 %fusion.3 = f32[2,64,129,128]{3,2,1,0:T(8,128)} fusion(f32[2,64,128,128]{3,2,1,0:T(8,128)S(1)} %bitcast.236, f32[2,64,1,128]{3,2,1,0:T(1,128)S(1)} %get-tuple-element.56, f32[2,64,1,128]{3,2,1,0:T(1,128)S(1)} %get-tuple-element.55, f32[2,64,1,128]{3,2,1,0:T(1,128)S(1)} %get-tuple-element.54, f32[2,64,128,128]{3,2,1,0:T(8,128)} %copy-done.1, ...), kind=kLoop, calls=%fused_computation.13 | loop fusion | flops 23248896 | bytes 25493504 | tf_op jit(solution)/shard_map/vmap()/add | solution.py:38
  201.1 25.7 %fusion.1 = f32[2,64,128,129]{3,2,1,0:T(8,128)} fusion(f32[2,64,128,128]{3,2,1,0:T(8,128)S(1)} %bitcast.236, f32[2,64,128,1]{3,2,1,0:T(8,128)} %get-tuple-element.52, f32[2,64,128,1]{3,2,1,0:T(8,128)} %get-tuple-element.51, f32[2,64,128,1]{3,2,1,0:T(8,128)} %get-tuple-element.50, f32[2,64,128,128]{3,2,1,0:T(8,128)} %get-tuple-element.78, ...), kind=kLoop, calls=%fused_computation.8 | loop fusion | flops 23248896 | bytes 25493504 | tf_op jit(solution)/shard_map/vmap()/add | solution.py:38
  226.8 22.0 %convert_bitcast_fusion = (bf16[2,1,64,128,128]{4,3,2,1,0:T(8,128)(2,1)}, f32[2,64,128,128]{3,2,1,0:T(8,128)}) fusion(f32[2,64,129,128]{3,2,1,0:T(8,128)} %fusion.3, f32[2,64,128,129]{3,2,1,0:T(8,128)} %fusion.1, bf16[2,1,64,128,128]{4,3,2,1,0:T(8,128)(2,1)} %param.7, f32[128,128]{1,0:T(8,128)S(1)} %get-tuple-element.81, f32[64]{0:T(128)S(1)} %fusion.129, ...), kind=kLoop, calls=%fused_computation.23 | loop fusion | flops 31457280 | bytes 50594048 | tf_op jit(solution)/shard_map/broadcast_in_dim | solution.py:223
  248.9 3.8 %reduce_sum.29 = f32[2,128,128]{2,1,0:T(8,128)S(1)} reduce(f32[2,64,128,128]{3,2,1,0:T(8,128)} %get-tuple-element.44, f32[]{:T(128)} %constant.200.clone.1), dimensions={1}, to_apply=%region_1.2 | reduce | flops 2064384 | bytes 8519684 | tf_op jit(solution)/shard_map/vmap()/reduce_sum | solution.py:63
  252.7 9.8 %add.508 = f32[2,64,2,64,2]{4,3,2,1,0:T(8,128)} reshape(f32[2,128,128]{2,1,0:T(8,128)S(1)} %multiply_add_fusion) | data formatting | bytes 262144 | tf_op jit(solution)/shard_map/vmap()/add | solution.py:63
  262.5 4.5 %reduce_sum.30 = f32[2,64,64]{2,1,0:T(8,128)S(1)} reduce(f32[2,64,2,64,2]{4,3,2,1,0:T(8,128)} %add.508, f32[]{:T(128)} %constant.200.clone.1), dimensions={2,4}, to_apply=%region_2.3 | reduce | flops 24576 | bytes 163844 | tf_op jit(solution)/shard_map/vmap()/reduce_sum | solution.py:64
  267.2 17.1 %all_gather.7 = bf16[2,16,4096]{2,0,1:T(2,128)(2,1)S(1)} all-gather(bf16[2,1,4096]{2,0,1:T(2,128)(2,1)S(1)} %convert_element_type.422), channel_id=1, replica_groups=mesh['wide'=16,'grp'=8] {'wide'}, dimensions={1}, use_global_device_ids=true | all-gather | bytes 278528 | tf_op jit(solution)/shard_map/all_gather | solution.py:191
  286.1 11.0 %all-to-all-start.2 = ((bf16[8,16,256]{2,1,0:T(8,128)(2,1)}), bf16[8,16,256]{2,1,0:T(8,128)(2,1)S(1)}, u32[]{:S(2)}, u32[]{:S(2)}) async-start(bf16[8,16,256]{2,1,0:T(8,128)(2,1)} %convert_element_type.425), calls=%async_computation.2 | async-start | bytes 131072 | tf_op jit(solution)/shard_map/all_to_all | solution.py:210
  297.5 4.4 %all-to-all-done.2 = bf16[8,16,256]{2,1,0:T(8,128)(2,1)S(1)} async-done(((bf16[8,16,256]{2,1,0:T(8,128)(2,1)}), bf16[8,16,256]{2,1,0:T(8,128)(2,1)S(1)}, u32[]{:S(2)}, u32[]{:S(2)}) %all-to-all-start.2) | async-done | bytes 65568 | tf_op jit(solution)/shard_map/all_to_all | solution.py:210
  307.2 4.9 %all-to-all-start.3 = ((bf16[128,2,256]{2,1,0:T(2,128)(2,1)}), bf16[128,2,256]{2,1,0:T(2,128)(2,1)S(1)}, u32[]{:S(2)}, u32[]{:S(2)}) async-start(bf16[128,2,256]{2,1,0:T(2,128)(2,1)} %reshape.531), calls=%async_computation.3 | async-start | bytes 262144 | tf_op jit(solution)/shard_map/all_to_all | solution.py:220
  312.8 9.3 %all-to-all-done.3 = bf16[128,2,256]{2,1,0:T(2,128)(2,1)S(1)} async-done(((bf16[128,2,256]{2,1,0:T(2,128)(2,1)}), bf16[128,2,256]{2,1,0:T(2,128)(2,1)S(1)}, u32[]{:S(2)}, u32[]{:S(2)}) %all-to-all-start.3) | async-done | bytes 131104 | tf_op jit(solution)/shard_map/all_to_all | solution.py:220
  322.7 2.0 copy.162
  (158 shorter events, 46.4 us)
Async XLA Ops:
  7.2 133.5 %all-gather.2.cloned.1.call-start = ((), (), s32[]{:S(2)}) async-start(), calls=%async_computation.4 | async-start | bytes 3342336 | tf_op jit(solution)/shard_map/all_gather | solution.py:176
  7.3 6.5 %copy-start.3 = (f32[32,64]{1,0:T(8,128)}, f32[32,64]{1,0:T(8,128)S(1)}, u32[]{:S(2)}) copy-start(f32[32,64]{1,0:T(8,128)S(1)} %get-tuple-element.88) | copy-start | bytes 24580
  62.6 7.6 %copy-start.2 = (bf16[3,16,128,16]{1,2,3,0:T(8,128)(2,1)S(1)}, bf16[3,16,128,16]{1,2,3,0:T(8,128)(2,1)}, u32[]{:S(2)}) copy-start(bf16[3,16,128,16]{1,2,3,0:T(8,128)(2,1)} %get-tuple-element.57) | copy-start | bytes 589828
  70.2 6.9 %copy-start.4 = (f32[32,64]{1,0:T(8,128)S(1)}, f32[32,64]{1,0:T(8,128)}, u32[]{:S(2)}) copy-start(f32[32,64]{1,0:T(8,128)} %copy-done.3) | copy-start | bytes 24580
  77.1 19.5 %copy-start.8 = (s32[256]{0:T(256)S(1)}, s32[256]{0:T(256)}, u32[]{:S(2)}) copy-start(s32[256]{0:T(256)} %param.6) | copy-start | bytes 3076
  151.7 0.7 copy-start.5
  157.5 8.4 %copy-start = (f32[2,64,128,128]{3,2,1,0:T(8,128)}, f32[2,64,128,128]{3,2,1,0:T(8,128)S(1)}, u32[]{:S(2)}) copy-start(f32[2,64,128,128]{3,2,1,0:T(8,128)S(1)} %fusion.8) | copy-start | bytes 25165828
  166.4 22.1 %slice-start = ((s8[8388608]{0:T(1024)(128)(4,1)}), s8[4194304]{0:T(1024)(128)(4,1)S(1)}, s32[]{:S(2)}) async-start(s8[8388608]{0:T(1024)(128)(4,1)} %bitcast.235), calls=%async_computation.5 | async-start | bytes 8388608
  171.9 3.2 copy-start.1
  175.2 13.3 %slice-start.1 = ((s8[8388608]{0:T(1024)(128)(4,1)}), s8[4194304]{0:T(1024)(128)(4,1)S(1)}, s32[]{:S(2)}) async-start(s8[8388608]{0:T(1024)(128)(4,1)} %bitcast.235), calls=%async_computation.6 | async-start | bytes 8388608
  252.7 32.5 %copy-start.7 = (pred[2,4]{1,0:T(4,128)(4,1)S(1)}, pred[2,4]{1,0:T(4,128)(4,1)}, u32[]{:S(2)}) copy-start(pred[2,4]{1,0:T(4,128)(4,1)} %broadcast_in_dim.29) | copy-start | bytes 28
  262.5 39.9 %copy-start.6 = (f32[32,64]{1,0:T(8,128)S(1)}, f32[32,64]{1,0:T(8,128)}, u32[]{:S(2)}) copy-start(f32[32,64]{1,0:T(8,128)} %get-tuple-element.93) | copy-start | bytes 24580
  286.1 15.8 %all-to-all-start.2 = ((bf16[8,16,256]{2,1,0:T(8,128)(2,1)}), bf16[8,16,256]{2,1,0:T(8,128)(2,1)S(1)}, u32[]{:S(2)}, u32[]{:S(2)}) async-start(bf16[8,16,256]{2,1,0:T(8,128)(2,1)} %convert_element_type.425), calls=%async_computation.2 | async-start | bytes 131072 | tf_op jit(solution)/shard_map/all_to_all | solution.py:210
  307.2 14.9 %all-to-all-start.3 = ((bf16[128,2,256]{2,1,0:T(2,128)(2,1)}), bf16[128,2,256]{2,1,0:T(2,128)(2,1)S(1)}, u32[]{:S(2)}, u32[]{:S(2)}) async-start(bf16[128,2,256]{2,1,0:T(2,128)(2,1)} %reshape.531), calls=%async_computation.3 | async-start | bytes 262144 | tf_op jit(solution)/shard_map/all_to_all | solution.py:220
Sparse Core Ops, SparseCore 0:
  96.7 44.0 all-gather.1
where the time goes:
time: 346 us; the launch traced here: 339 us
  local copies, waits for them, and re-layouts  104 us (30%)
  other arithmetic  86.5 us (25%)
  waiting for transfers between devices  53.3 us (15%)
  blocking collectives  50.5 us (15%)
  starting transfers between devices  16 us (5%)
  between operations  15.4 us (4%)
  matrix products  13 us (4%)
    all_gather x1, waiting for transfers between devices, shards(): lax.all_gather(band_fields.astype(jnp.bfloat16), 'wide', axis=1, tiled=True)  39.6 us
    add x2, other arithmetic, upwind_flux(): jnp.maximum(face_speed, 0.0) * left_vals  38.3 us
    all_to_all x1, blocking collectives, shards(): lax.all_to_all(inverse_rows, ('wide', 'grp'), split_axis=1, concat_axis=2...  24.1 us
    broadcast_in_dim x1, other arithmetic, shards(): return (surface, new_states[:, None], tendency)  22 us
    unnamed x33, local copies, waits for them, and re-layouts  21.2 us
    all_gather x1, blocking collectives, shards(): lax.all_gather(coarse_flat.reshape(2, 1, TS * TS).astype(jnp.bfloat16), '...  17.1 us
    slice x2, local copies, waits for them, and re-layouts, upwind_flux(): speed_pad = jnp.pad(speeds, widths, mode='edge')  13.4 us
    dot_general x28, matrix products, contract(): return jnp.einsum(pattern, data, table, preferred_element_type=jnp.float32)  13 us
  transfers between devices with their start and end apart: 3, of which 3 were waited for; matrix products, arithmetic and copies ran while one was open for 2% of the time, Pallas kernels for 0%

commit v1 on v0

--- a/solution.py
+++ b/solution.py
@@ -10,6 +10,27 @@
 Z_TOP = 2.0
 DECAY_RATE = 0.5
 COURANT = 0.3
+
+
+def gather_around(shard, axis, dim):
+    size, index, extent = (lax.axis_size(axis), lax.axis_index(axis), shard.shape[dim])
+    forward = [(i, (i + 1) % size) for i in range(size)]
+    left = [(i, (i - 1) % size) for i in range(size)]
+    out = jnp.zeros((*shard.shape[:dim], size * extent, *shard.shape[dim + 1 :]), shard.dtype)
+    out = lax.dynamic_update_slice_in_dim(out, shard, index * extent, axis=dim)
+    from_left = from_right = shard
+    half = size // 2
+    for step in range(1, half + 1):
+        from_left = lax.ppermute(from_left, axis, forward)
+        out = lax.dynamic_update_slice_in_dim(
+            out, from_left, (index - step) % size * extent, axis=dim
+        )
+        if step < size - half:
+            from_right = lax.ppermute(from_right, axis, left)
+            out = lax.dynamic_update_slice_in_dim(
+                out, from_right, (index + step) % size * extent, axis=dim
+            )
+    return out
 
 
 def for_sending(shard):
@@ -173,9 +194,9 @@
     rank_index = jnp.sum(
         jnp.where(matches, jnp.arange(per_group, dtype=jnp.int32)[None, :], 0), axis=1
     )
-    column_strip = lax.all_gather(
-        band_fields.astype(jnp.bfloat16), "wide", axis=1, tiled=True
-    ).astype(band_fields.dtype)
+    column_strip = gather_around(band_fields.astype(jnp.bfloat16), "wide", 1).astype(
+        band_fields.dtype
+    )
 
     def pick_strip(rank):
         return lax.dynamic_slice(

time: 346 us -> 362 us (1.046)
  starting transfers between devices: 16 us -> 72.6 us
  blocking collectives: 50.5 us -> 15.6 us
  between operations: 15.4 us -> 1.95 us
  waiting for transfers between devices: 53.3 us -> 59.7 us
    all_gather x1 -> x0, waiting for transfers between devices: 39.6 us -> none  [shards(): lax.all_gather(band_fields.astype(jnp.bfloat16), 'wide', axis=1, tiled=True)]
    ppermute x0 -> x15, waiting for transfers between devices: none -> 33.4 us  [the longest x8 19.5 us: gather_around(): from_left = lax.ppermute(from_left, axis, forward)]
    all_to_all x2 -> x0, blocking collectives: 33.4 us -> none  [the longest x1 24.1 us: shards(): lax.all_to_all(inverse_rows, ('wide', 'grp'), split_axis=1, concat_axis=2...]
    ppermute x0 -> x15, starting transfers between devices: none -> 31.8 us  [the longest x7 30.4 us: gather_around(): from_right = lax.ppermute(from_right, axis, left)]
    all_to_all x0 -> x2, starting transfers between devices: none -> 15.9 us  [the longest x1 11.8 us: shards(): lax.all_to_all(inverse_rows, ('wide', 'grp'), split_axis=1, concat_axis=2...]
    all_to_all x0 -> x2, waiting for transfers between devices: none -> 12.5 us  [the longest x1 6.68 us: shards(): lax.all_to_all(inverse_rows, ('wide', 'grp'), split_axis=1, concat_axis=2...]
    all_to_all x1, starting transfers between devices: 11 us -> 18.2 us  [shards(): lax.all_to_all(for_sending(surface_band), 'grp', split_axis=0, concat_axi...]
    unnamed x33 -> x41, local copies, waits for them, and re-layouts: 21.2 us -> 22.6 us
  transfers between devices with their start and end apart: 3 -> 19, of which waited for: 3 -> 13; matrix products, arithmetic and copies ran while one was open for 2% -> 3% of each run, Pallas kernels for 0% -> 0%
where the time goes in v1:
time: 362 us; the launch traced here: 355 us
  local copies, waits for them, and re-layouts  106 us (29%)
  other arithmetic  86.5 us (24%)
  starting transfers between devices  72.6 us (20%)
  waiting for transfers between devices  59.7 us (16%)
  blocking collectives  15.6 us (4%)
  matrix products  12.9 us (4%)
    add x2, other arithmetic, upwind_flux(): jnp.maximum(face_speed, 0.0) * left_vals  38.2 us
    ppermute x7, starting transfers between devices, gather_around(): from_right = lax.ppermute(from_right, axis, left)  30.4 us
    unnamed x41, local copies, waits for them, and re-layouts  22.6 us
    broadcast_in_dim x1, other arithmetic, shards(): return (surface, new_states[:, None], tendency)  22.2 us
    ppermute x8, waiting for transfers between devices, gather_around(): from_left = lax.ppermute(from_left, axis, forward)  19.5 us
    all_to_all x1, starting transfers between devices, shards(): lax.all_to_all(for_sending(surface_band), 'grp', split_axis=0, concat_axi...  18.2 us
    all_gather x1, blocking collectives, shards(): lax.all_gather(coarse_flat.reshape(2, 1, TS * TS).astype(jnp.bfloat16), '...  15.6 us
    ppermute x7, waiting for transfers between devices, gather_around(): from_right = lax.ppermute(from_right, axis, left)  13.9 us
  transfers between devices with their start and end apart: 19, of which 13 were waited for; matrix products, arithmetic and copies ran while one was open for 3% of the time, Pallas kernels for 0%

profile of v1, /device:TPU:1, one launch (start us, length us, event | category | flops | bytes accessed | tf_op | source)
XLA Modules:
  0.0 355.4 jit_solution(1812687824189227377)
XLA Ops:
  9.3 4.1 %copy.124 = bf16[6,2048,16]{2,0,1:T(8,128)(2,1)} copy(bf16[6,2048,16]{1,2,0:T(8,128)(2,1)S(1)} %maximum_bitcast_fusion) | data formatting | bytes 786432 | tf_op jit(solution)/shard_map/transpose | solution.py:168
  13.4 6.3 %reshape.527 = bf16[128,2,768]{2,1,0:T(2,128)(2,1)} reshape(bf16[2048,6,16]{2,1,0:T(8,128)(2,1)} %bitcast.240) | data formatting | bytes 786432
  19.7 11.8 %all-to-all-start = ((bf16[128,2,768]{2,1,0:T(2,128)(2,1)}), bf16[128,2,768]{2,1,0:T(2,128)(2,1)S(1)}, u32[]{:S(2)}, u32[]{:S(2)}) async-start(bf16[128,2,768]{2,1,0:T(2,128)(2,1)} %reshape.527), calls=%async_computation | async-start | bytes 786432 | tf_op jit(solution)/shard_map/all_to_all | solution.py:171
  37.0 6.7 %all-to-all-done = bf16[128,2,768]{2,1,0:T(2,128)(2,1)S(1)} async-done(((bf16[128,2,768]{2,1,0:T(2,128)(2,1)}), bf16[128,2,768]{2,1,0:T(2,128)(2,1)S(1)}, u32[]{:S(2)}, u32[]{:S(2)}) %all-to-all-start) | async-done | bytes 393248 | tf_op jit(solution)/shard_map/all_to_all | solution.py:171
  43.7 4.8 %reshape.528 = bf16[2048,6,16]{2,1,0:T(8,128)(2,1)} reshape(bf16[128,2,768]{2,1,0:T(2,128)(2,1)S(1)} %all-to-all-done) | data formatting | bytes 786432
  48.5 6.1 %copy.158 = bf16[6,128,16,16]{2,1,3,0:T(8,128)(2,1)S(1)} copy(bf16[6,128,16,16]{3,0,2,1:T(8,128)(2,1)} %bitcast.239) | data formatting | bytes 786432 | tf_op jit(solution)/shard_map/all_to_all | solution.py:171
  56.6 4.3 %copy.126 = bf16[3,16,128,16]{3,2,1,0:T(8,128)(2,1)S(1)} copy(bf16[3,16,128,16]{1,2,3,0:T(8,128)(2,1)} %get-tuple-element.58) | data formatting | bytes 393216 | tf_op jit(solution)/shard_map/slice | solution.py:172
  77.9 4.2 %all-to-all-start.1 = ((bf16[8,2,6144]{2,1,0:T(2,128)(2,1)}), bf16[8,2,6144]{2,1,0:T(2,128)(2,1)S(1)}, u32[]{:S(2)}, u32[]{:S(2)}) async-start(bf16[8,2,6144]{2,1,0:T(2,128)(2,1)} %reshape.529), calls=%async_computation.1 | async-start | bytes 393216 | tf_op jit(solution)/shard_map/all_to_all | solution.py:173
  82.2 5.8 %all-to-all-done.1 = bf16[8,2,6144]{2,1,0:T(2,128)(2,1)S(1)} async-done(((bf16[8,2,6144]{2,1,0:T(2,128)(2,1)}), bf16[8,2,6144]{2,1,0:T(2,128)(2,1)S(1)}, u32[]{:S(2)}, u32[]{:S(2)}) %all-to-all-start.1) | async-done | bytes 196640 | tf_op jit(solution)/shard_map/all_to_all | solution.py:173
  96.6 3.8 %collective-permute-start.3 = (bf16[3,128,256]{2,1,0:T(8,128)(2,1)}, bf16[3,128,256]{2,1,0:T(8,128)(2,1)S(1)}, u32[]{:S(2)}, u32[]{:S(2)}) collective-permute-start(bf16[3,128,256]{2,1,0:T(8,128)(2,1)} %collective-permute-done.1), channel_id=1, source_target_pairs={{0,120},{8,0},{16,8},{24,16},{32,24},{40,32},{48,40},{56,48},{64,5... | collective-permute-start | bytes 589832 | tf_op jit(solution)/shard_map/ppermute | solution.py:29
  103.3 5.1 %collective-permute-start.5 = (bf16[3,128,256]{2,1,0:T(8,128)(2,1)S(1)}, bf16[3,128,256]{2,1,0:T(8,128)(2,1)S(1)}, u32[]{:S(2)}, u32[]{:S(2)}) collective-permute-start(bf16[3,128,256]{2,1,0:T(8,128)(2,1)S(1)} %collective-permute-done.3), channel_id=1, source_target_pairs={{0,120},{8,0},{16,8},{24,16},{32,24},{40,32},{48,40},{56,48},{64,5... | collective-permute-start | bytes 589832 | tf_op jit(solution)/shard_map/ppermute | solution.py:29
  111.0 5.2 %collective-permute-start.7 = (bf16[3,128,256]{2,1,0:T(8,128)(2,1)S(1)}, bf16[3,128,256]{2,1,0:T(8,128)(2,1)S(1)}, u32[]{:S(2)}, u32[]{:S(2)}) collective-permute-start(bf16[3,128,256]{2,1,0:T(8,128)(2,1)S(1)} %collective-permute-done.5), channel_id=1, source_target_pairs={{0,120},{8,0},{16,8},{24,16},{32,24},{40,32},{48,40},{56,48},{64,5... | collective-permute-start | bytes 589832 | tf_op jit(solution)/shard_map/ppermute | solution.py:29
  118.9 5.2 %collective-permute-start.9 = (bf16[3,128,256]{2,1,0:T(8,128)(2,1)S(1)}, bf16[3,128,256]{2,1,0:T(8,128)(2,1)S(1)}, u32[]{:S(2)}, u32[]{:S(2)}) collective-permute-start(bf16[3,128,256]{2,1,0:T(8,128)(2,1)S(1)} %collective-permute-done.7), channel_id=1, source_target_pairs={{0,120},{8,0},{16,8},{24,16},{32,24},{40,32},{48,40},{56,48},{64,5... | collective-permute-start | bytes 589832 | tf_op jit(solution)/shard_map/ppermute | solution.py:29
  126.7 5.2 %collective-permute-start.11 = (bf16[3,128,256]{2,1,0:T(8,128)(2,1)S(1)}, bf16[3,128,256]{2,1,0:T(8,128)(2,1)S(1)}, u32[]{:S(2)}, u32[]{:S(2)}) collective-permute-start(bf16[3,128,256]{2,1,0:T(8,128)(2,1)S(1)} %collective-permute-done.9), channel_id=1, source_target_pairs={{0,120},{8,0},{16,8},{24,16},{32,24},{40,32},{48,40},{56,48},{64,5... | collective-permute-start | bytes 589832 | tf_op jit(solution)/shard_map/ppermute | solution.py:29
  134.6 5.2 %collective-permute-start.13 = (bf16[3,128,256]{2,1,0:T(8,128)(2,1)S(1)}, bf16[3,128,256]{2,1,0:T(8,128)(2,1)S(1)}, u32[]{:S(2)}, u32[]{:S(2)}) collective-permute-start(bf16[3,128,256]{2,1,0:T(8,128)(2,1)S(1)} %collective-permute-done.11), channel_id=1, source_target_pairs={{0,120},{8,0},{16,8},{24,16},{32,24},{40,32},{48,40},{56,48},{64,5... | collective-permute-start | bytes 589832 | tf_op jit(solution)/shard_map/ppermute | solution.py:29
  140.2 9.2 %collective-permute-done.12 = bf16[3,128,256]{2,1,0:T(8,128)(2,1)S(1)} collective-permute-done((bf16[3,128,256]{2,1,0:T(8,128)(2,1)S(1)}, bf16[3,128,256]{2,1,0:T(8,128)(2,1)S(1)}, u32[]{:S(2)}, u32[]{:S(2)}) %collective-permute-start.12) | collective-permute-done | bytes 196640 | tf_op jit(solution)/shard_map/ppermute | solution.py:24
  149.8 10.1 %collective-permute-done.14 = bf16[3,128,256]{2,1,0:T(8,128)(2,1)S(1)} collective-permute-done((bf16[3,128,256]{2,1,0:T(8,128)(2,1)S(1)}, bf16[3,128,256]{2,1,0:T(8,128)(2,1)S(1)}, u32[]{:S(2)}, u32[]{:S(2)}) %collective-permute-start.14) | collective-permute-done | bytes 196640 | tf_op jit(solution)/shard_map/ppermute | solution.py:24
  163.1 5.9 %while.1 = (s32[]{:T(128)}, f32[3,2048,256]{2,1,0:T(8,128)}, s32[2,3]{1,0:T(2,128)S(1)}, f32[2,3,64,64]{3,2,1,0:T(8,128)S(1)}, s32[]{:T(128)}) while((s32[]{:T(128)}, f32[3,2048,256]{2,1,0:T(8,128)}, s32[2,3]{1,0:T(2,128)S(1)}, f32[2,3,64,64]{3,2,1,0:T(8,128)S(1)}, s32[]{:T(128)}) %tuple.59), condition=%wide.while_cond, body=%wide.while_body.sunk | while | flops 2 | bytes 147581 | solution.py:202
  169.4 3.9 %fusion.8 = f32[2,64,128,128]{3,2,1,0:T(8,128)S(1)} fusion(bf16[2,1,64,128,128]{4,3,2,1,0:T(8,128)(2,1)} %param.7, f32[128,128]{1,0:T(8,128)S(1)} %get-tuple-element.81, f32[64]{0:T(128)S(1)} %copy-done.8, f32[2,128,128]{2,1,0:T(8,128)S(1)} %copy.134, f32[128,128]{1,0:T(8,128)S(1)} %get-tuple-element.80), kind=kLoop, calls=%fused_computation.22 | loop fusion | flops 16777216 | bytes 12845312 | tf_op jit(solution)/shard_map/vmap()/add | solution.py:76
  173.4 7.7 %fusion.246 = (f32[2,64,128,1]{3,2,1,0:T(8,128)}, f32[2,64,128,1]{3,2,1,0:T(8,128)}) fusion(f32[2,64,128,128]{3,2,1,0:T(8,128)S(1)} %fusion.8), kind=kLoop, calls=%fused_computation.369 | loop fusion | bytes 262144 | tf_op jit(solution)/shard_map/vmap(jit(_pad))/slice | solution.py:50
  182.3 5.4 %broadcast_multiply_fusion.1 = (f32[2,64,128,128]{3,2,1,0:T(8,128)}, f32[2,64,128,128]{3,2,1,0:T(8,128)S(1)}) fusion(f32[64]{0:T(128)S(1)} %multiply_exponential_fusion, f32[2,128,128]{2,1,0:T(8,128)S(1)} %copy.137, f32[2,128,128]{2,1,0:T(8,128)S(1)} %copy.139), kind=kLoop, calls=%fused_computation.25 | loop fusion | flops 4194304 | bytes 17039616 | tf_op jit(solution)/shard_map/vmap()/mul | solution.py:78
  191.1 13.4 %fusion.245 = (f32[2,64,128,1]{3,2,1,0:T(8,128)}, f32[2,64,128,1]{3,2,1,0:T(8,128)}) fusion(f32[2,64,128,128]{3,2,1,0:T(8,128)} %get-tuple-element.78), kind=kLoop, calls=%fused_computation.368 | loop fusion | bytes 262144 | tf_op jit(solution)/shard_map/vmap(jit(_pad))/slice | solution.py:51
  204.5 12.6 %fusion.3 = f32[2,64,129,128]{3,2,1,0:T(8,128)} fusion(f32[2,64,128,128]{3,2,1,0:T(8,128)S(1)} %bitcast.236, f32[2,64,1,128]{3,2,1,0:T(1,128)S(1)} %get-tuple-element.56, f32[2,64,1,128]{3,2,1,0:T(1,128)S(1)} %get-tuple-element.55, f32[2,64,1,128]{3,2,1,0:T(1,128)S(1)} %get-tuple-element.54, f32[2,64,128,128]{3,2,1,0:T(8,128)} %copy-done.1, ...), kind=kLoop, calls=%fused_computation.13 | loop fusion | flops 23248896 | bytes 25493504 | tf_op jit(solution)/shard_map/vmap()/add | solution.py:59
  217.1 25.6 %fusion.1 = f32[2,64,128,129]{3,2,1,0:T(8,128)} fusion(f32[2,64,128,128]{3,2,1,0:T(8,128)S(1)} %bitcast.236, f32[2,64,128,1]{3,2,1,0:T(8,128)} %get-tuple-element.52, f32[2,64,128,1]{3,2,1,0:T(8,128)} %get-tuple-element.51, f32[2,64,128,1]{3,2,1,0:T(8,128)} %get-tuple-element.50, f32[2,64,128,128]{3,2,1,0:T(8,128)} %get-tuple-element.78, ...), kind=kLoop, calls=%fused_computation.8 | loop fusion | flops 23248896 | bytes 25493504 | tf_op jit(solution)/shard_map/vmap()/add | solution.py:59
  242.7 22.2 %convert_bitcast_fusion = (bf16[2,1,64,128,128]{4,3,2,1,0:T(8,128)(2,1)}, f32[2,64,128,128]{3,2,1,0:T(8,128)}) fusion(f32[2,64,129,128]{3,2,1,0:T(8,128)} %fusion.3, f32[2,64,128,129]{3,2,1,0:T(8,128)} %fusion.1, bf16[2,1,64,128,128]{4,3,2,1,0:T(8,128)(2,1)} %param.7, f32[128,128]{1,0:T(8,128)S(1)} %get-tuple-element.81, f32[64]{0:T(128)S(1)} %copy-done.8, ...), kind=kLoop, calls=%fused_computation.23 | loop fusion | flops 31457280 | bytes 50594048 | tf_op jit(solution)/shard_map/broadcast_in_dim | solution.py:244
  268.7 9.8 %add.669 = f32[2,64,2,64,2]{4,3,2,1,0:T(8,128)} reshape(f32[2,128,128]{2,1,0:T(8,128)S(1)} %multiply_add_fusion) | data formatting | bytes 262144 | tf_op jit(solution)/shard_map/vmap()/add | solution.py:84
  278.5 4.6 %reduce_sum.30 = f32[2,64,64]{2,1,0:T(8,128)S(1)} reduce(f32[2,64,2,64,2]{4,3,2,1,0:T(8,128)} %add.669, f32[]{:T(128)} %constant.280.clone.1), dimensions={2,4}, to_apply=%region_2.3 | reduce | flops 24576 | bytes 163844 | tf_op jit(solution)/shard_map/vmap()/reduce_sum | solution.py:85
  283.2 15.6 %all_gather.3 = bf16[2,16,4096]{2,0,1:T(2,128)(2,1)S(1)} all-gather(bf16[2,1,4096]{2,0,1:T(2,128)(2,1)S(1)} %convert_element_type.422), channel_id=1, replica_groups=mesh['wide'=16,'grp'=8] {'wide'}, dimensions={1}, use_global_device_ids=true | all-gather | bytes 278528 | tf_op jit(solution)/shard_map/all_gather | solution.py:212
  300.7 18.2 %all-to-all-start.2 = ((bf16[8,16,256]{2,1,0:T(8,128)(2,1)}), bf16[8,16,256]{2,1,0:T(8,128)(2,1)S(1)}, u32[]{:S(2)}, u32[]{:S(2)}) async-start(bf16[8,16,256]{2,1,0:T(8,128)(2,1)} %convert_element_type.425), calls=%async_computation.2 | async-start | bytes 131072 | tf_op jit(solution)/shard_map/all_to_all | solution.py:231
  319.3 4.5 %all-to-all-done.2 = bf16[8,16,256]{2,1,0:T(8,128)(2,1)S(1)} async-done(((bf16[8,16,256]{2,1,0:T(8,128)(2,1)}), bf16[8,16,256]{2,1,0:T(8,128)(2,1)S(1)}, u32[]{:S(2)}, u32[]{:S(2)}) %all-to-all-start.2) | async-done | bytes 65568 | tf_op jit(solution)/shard_map/all_to_all | solution.py:231
  329.1 6.7 %all-to-all-start.3 = ((bf16[128,2,256]{2,1,0:T(2,128)(2,1)}), bf16[128,2,256]{2,1,0:T(2,128)(2,1)S(1)}, u32[]{:S(2)}, u32[]{:S(2)}) async-start(bf16[128,2,256]{2,1,0:T(2,128)(2,1)} %reshape.531), calls=%async_computation.3 | async-start | bytes 262144 | tf_op jit(solution)/shard_map/all_to_all | solution.py:241
  336.4 9.3 %all-to-all-done.3 = bf16[128,2,256]{2,1,0:T(2,128)(2,1)S(1)} async-done(((bf16[128,2,256]{2,1,0:T(2,128)(2,1)}), bf16[128,2,256]{2,1,0:T(2,128)(2,1)S(1)}, u32[]{:S(2)}, u32[]{:S(2)}) %all-to-all-start.3) | async-done | bytes 131104 | tf_op jit(solution)/shard_map/all_to_all | solution.py:241
  (212 shorter events, 90.9 us)
Async XLA Ops:
  6.4 25.1 %copy-start.12 = (s32[256]{0:T(256)S(1)}, s32[256]{0:T(256)}, u32[]{:S(2)}) copy-start(s32[256]{0:T(256)} %param.6) | copy-start | bytes 3076
  19.7 24.0 %all-to-all-start = ((bf16[128,2,768]{2,1,0:T(2,128)(2,1)}), bf16[128,2,768]{2,1,0:T(2,128)(2,1)S(1)}, u32[]{:S(2)}, u32[]{:S(2)}) async-start(bf16[128,2,768]{2,1,0:T(2,128)(2,1)} %reshape.527), calls=%async_computation | async-start | bytes 786432 | tf_op jit(solution)/shard_map/all_to_all | solution.py:171
  56.6 7.5 %copy-start.2 = (bf16[3,16,128,16]{1,2,3,0:T(8,128)(2,1)S(1)}, bf16[3,16,128,16]{1,2,3,0:T(8,128)(2,1)}, u32[]{:S(2)}) copy-start(bf16[3,16,128,16]{1,2,3,0:T(8,128)(2,1)} %get-tuple-element.57) | copy-start | bytes 589828
  64.1 6.9 %copy-start.4 = (f32[32,64]{1,0:T(8,128)S(1)}, f32[32,64]{1,0:T(8,128)}, u32[]{:S(2)}) copy-start(f32[32,64]{1,0:T(8,128)} %copy-done.3) | copy-start | bytes 24580
  67.3 14.8 %copy-start.9 = (f32[128]{0:T(128)S(1)}, f32[128]{0:T(128)}, u32[]{:S(2)}) copy-start(f32[128]{0:T(128)} %subtract_minimum_fusion) | copy-start | bytes 1540
  77.9 10.1 %all-to-all-start.1 = ((bf16[8,2,6144]{2,1,0:T(2,128)(2,1)}), bf16[8,2,6144]{2,1,0:T(2,128)(2,1)S(1)}, u32[]{:S(2)}, u32[]{:S(2)}) async-start(bf16[8,2,6144]{2,1,0:T(2,128)(2,1)} %reshape.529), calls=%async_computation.1 | async-start | bytes 393216 | tf_op jit(solution)/shard_map/all_to_all | solution.py:173
  90.9 5.6 %collective-permute-start.1 = (bf16[3,128,256]{2,1,0:T(8,128)(2,1)S(1)}, bf16[3,128,256]{2,1,0:T(8,128)(2,1)}, u32[]{:S(2)}, u32[]{:S(2)}) collective-permute-start(bf16[3,128,256]{2,1,0:T(8,128)(2,1)S(1)} %bitcast.247), channel_id=1, source_target_pairs={{0,120},{8,0},{16,8},{24,16},{32,24},{40,32},{48,40},{56,48},{64,5... | collective-permute-start | bytes 589832 | tf_op jit(solution)/shard_map/ppermute | solution.py:29
  91.5 8.9 %collective-permute-start = (bf16[3,128,256]{2,1,0:T(8,128)(2,1)S(1)}, bf16[3,128,256]{2,1,0:T(8,128)(2,1)}, u32[]{:S(2)}, u32[]{:S(2)}) collective-permute-start(bf16[3,128,256]{2,1,0:T(8,128)(2,1)S(1)} %bitcast.248), channel_id=1, source_target_pairs={{0,8},{8,16},{16,24},{24,32},{32,40},{40,48},{48,56},{56,64},{64,7... | collective-permute-start | bytes 589832 | tf_op jit(solution)/shard_map/ppermute | solution.py:24
  93.9 69.2 %copy-start.5 = (f32[2,3,64,64]{3,2,1,0:T(8,128)S(1)}, f32[2,3,64,64]{3,2,1,0:T(8,128)}, u32[]{:S(2)}) copy-start(f32[2,3,64,64]{3,2,1,0:T(8,128)} %custom-call.8) | copy-start | bytes 294916
  93.9 69.2 %copy-start.10 = (s32[2,3]{1,0:T(2,128)S(1)}, s32[2,3]{1,0:T(2,128)}, u32[]{:S(2)}) copy-start(s32[2,3]{1,0:T(2,128)} %copy.132) | copy-start | bytes 76
  96.6 6.7 %collective-permute-start.3 = (bf16[3,128,256]{2,1,0:T(8,128)(2,1)}, bf16[3,128,256]{2,1,0:T(8,128)(2,1)S(1)}, u32[]{:S(2)}, u32[]{:S(2)}) collective-permute-start(bf16[3,128,256]{2,1,0:T(8,128)(2,1)} %collective-permute-done.1), channel_id=1, source_target_pairs={{0,120},{8,0},{16,8},{24,16},{32,24},{40,32},{48,40},{56,48},{64,5... | collective-permute-start | bytes 589832 | tf_op jit(solution)/shard_map/ppermute | solution.py:29
  100.4 8.1 %collective-permute-start.2 = (bf16[3,128,256]{2,1,0:T(8,128)(2,1)}, bf16[3,128,256]{2,1,0:T(8,128)(2,1)S(1)}, u32[]{:S(2)}, u32[]{:S(2)}) collective-permute-start(bf16[3,128,256]{2,1,0:T(8,128)(2,1)} %collective-permute-done), channel_id=1, source_target_pairs={{0,8},{8,16},{16,24},{24,32},{32,40},{40,48},{48,56},{56,64},{64,7... | collective-permute-start | bytes 589832 | tf_op jit(solution)/shard_map/ppermute | solution.py:24
  103.3 7.7 %collective-permute-start.5 = (bf16[3,128,256]{2,1,0:T(8,128)(2,1)S(1)}, bf16[3,128,256]{2,1,0:T(8,128)(2,1)S(1)}, u32[]{:S(2)}, u32[]{:S(2)}) collective-permute-start(bf16[3,128,256]{2,1,0:T(8,128)(2,1)S(1)} %collective-permute-done.3), channel_id=1, source_target_pairs={{0,120},{8,0},{16,8},{24,16},{32,24},{40,32},{48,40},{56,48},{64,5... | collective-permute-start | bytes 589832 | tf_op jit(solution)/shard_map/ppermute | solution.py:29
  108.4 7.8 %collective-permute-start.4 = (bf16[3,128,256]{2,1,0:T(8,128)(2,1)S(1)}, bf16[3,128,256]{2,1,0:T(8,128)(2,1)S(1)}, u32[]{:S(2)}, u32[]{:S(2)}) collective-permute-start(bf16[3,128,256]{2,1,0:T(8,128)(2,1)S(1)} %collective-permute-done.2), channel_id=1, source_target_pairs={{0,8},{8,16},{16,24},{24,32},{32,40},{40,48},{48,56},{56,64},{64,7... | collective-permute-start | bytes 589832 | tf_op jit(solution)/shard_map/ppermute | solution.py:24
  108.5 60.9 %copy-start.8 = (f32[64]{0:T(128)S(1)}, f32[64]{0:T(128)}, u32[]{:S(2)}) copy-start(f32[64]{0:T(128)} %fusion.157) | copy-start | bytes 772
  111.0 7.8 %collective-permute-start.7 = (bf16[3,128,256]{2,1,0:T(8,128)(2,1)S(1)}, bf16[3,128,256]{2,1,0:T(8,128)(2,1)S(1)}, u32[]{:S(2)}, u32[]{:S(2)}) collective-permute-start(bf16[3,128,256]{2,1,0:T(8,128)(2,1)S(1)} %collective-permute-done.5), channel_id=1, source_target_pairs={{0,120},{8,0},{16,8},{24,16},{32,24},{40,32},{48,40},{56,48},{64,5... | collective-permute-start | bytes 589832 | tf_op jit(solution)/shard_map/ppermute | solution.py:29
  116.3 7.8 %collective-permute-start.6 = (bf16[3,128,256]{2,1,0:T(8,128)(2,1)S(1)}, bf16[3,128,256]{2,1,0:T(8,128)(2,1)S(1)}, u32[]{:S(2)}, u32[]{:S(2)}) collective-permute-start(bf16[3,128,256]{2,1,0:T(8,128)(2,1)S(1)} %collective-permute-done.4), channel_id=1, source_target_pairs={{0,8},{8,16},{16,24},{24,32},{32,40},{40,48},{48,56},{56,64},{64,7... | collective-permute-start | bytes 589832 | tf_op jit(solution)/shard_map/ppermute | solution.py:24
  118.9 7.8 %collective-permute-start.9 = (bf16[3,128,256]{2,1,0:T(8,128)(2,1)S(1)}, bf16[3,128,256]{2,1,0:T(8,128)(2,1)S(1)}, u32[]{:S(2)}, u32[]{:S(2)}) collective-permute-start(bf16[3,128,256]{2,1,0:T(8,128)(2,1)S(1)} %collective-permute-done.7), channel_id=1, source_target_pairs={{0,120},{8,0},{16,8},{24,16},{32,24},{40,32},{48,40},{56,48},{64,5... | collective-permute-start | bytes 589832 | tf_op jit(solution)/shard_map/ppermute | solution.py:29
  124.1 7.8 %collective-permute-start.8 = (bf16[3,128,256]{2,1,0:T(8,128)(2,1)S(1)}, bf16[3,128,256]{2,1,0:T(8,128)(2,1)S(1)}, u32[]{:S(2)}, u32[]{:S(2)}) collective-permute-start(bf16[3,128,256]{2,1,0:T(8,128)(2,1)S(1)} %collective-permute-done.6), channel_id=1, source_target_pairs={{0,8},{8,16},{16,24},{24,32},{32,40},{40,48},{48,56},{56,64},{64,7... | collective-permute-start | bytes 589832 | tf_op jit(solution)/shard_map/ppermute | solution.py:24
  126.7 7.9 %collective-permute-start.11 = (bf16[3,128,256]{2,1,0:T(8,128)(2,1)S(1)}, bf16[3,128,256]{2,1,0:T(8,128)(2,1)S(1)}, u32[]{:S(2)}, u32[]{:S(2)}) collective-permute-start(bf16[3,128,256]{2,1,0:T(8,128)(2,1)S(1)} %collective-permute-done.9), channel_id=1, source_target_pairs={{0,120},{8,0},{16,8},{24,16},{32,24},{40,32},{48,40},{56,48},{64,5... | collective-permute-start | bytes 589832 | tf_op jit(solution)/shard_map/ppermute | solution.py:29
  132.0 8.2 %collective-permute-start.10 = (bf16[3,128,256]{2,1,0:T(8,128)(2,1)S(1)}, bf16[3,128,256]{2,1,0:T(8,128)(2,1)S(1)}, u32[]{:S(2)}, u32[]{:S(2)}) collective-permute-start(bf16[3,128,256]{2,1,0:T(8,128)(2,1)S(1)} %collective-permute-done.8), channel_id=1, source_target_pairs={{0,8},{8,16},{16,24},{24,32},{32,40},{40,48},{48,56},{56,64},{64,7... | collective-permute-start | bytes 589832 | tf_op jit(solution)/shard_map/ppermute | solution.py:24
  134.6 15.2 %collective-permute-start.13 = (bf16[3,128,256]{2,1,0:T(8,128)(2,1)S(1)}, bf16[3,128,256]{2,1,0:T(8,128)(2,1)S(1)}, u32[]{:S(2)}, u32[]{:S(2)}) collective-permute-start(bf16[3,128,256]{2,1,0:T(8,128)(2,1)S(1)} %collective-permute-done.11), channel_id=1, source_target_pairs={{0,120},{8,0},{16,8},{24,16},{32,24},{40,32},{48,40},{56,48},{64,5... | collective-permute-start | bytes 589832 | tf_op jit(solution)/shard_map/ppermute | solution.py:29
  140.1 9.2 %collective-permute-start.12 = (bf16[3,128,256]{2,1,0:T(8,128)(2,1)S(1)}, bf16[3,128,256]{2,1,0:T(8,128)(2,1)S(1)}, u32[]{:S(2)}, u32[]{:S(2)}) collective-permute-start(bf16[3,128,256]{2,1,0:T(8,128)(2,1)S(1)} %collective-permute-done.10), channel_id=1, source_target_pairs={{0,8},{8,16},{16,24},{24,32},{32,40},{40,48},{48,56},{56,64},{64,7... | collective-permute-start | bytes 589832 | tf_op jit(solution)/shard_map/ppermute | solution.py:24
  149.4 10.5 %collective-permute-start.14 = (bf16[3,128,256]{2,1,0:T(8,128)(2,1)S(1)}, bf16[3,128,256]{2,1,0:T(8,128)(2,1)S(1)}, u32[]{:S(2)}, u32[]{:S(2)}) collective-permute-start(bf16[3,128,256]{2,1,0:T(8,128)(2,1)S(1)} %collective-permute-done.12), channel_id=1, source_target_pairs={{0,8},{8,16},{16,24},{24,32},{32,40},{40,48},{48,56},{56,64},{64,7... | collective-permute-start | bytes 589832 | tf_op jit(solution)/shard_map/ppermute | solution.py:24
  173.3 8.4 %copy-start = (f32[2,64,128,128]{3,2,1,0:T(8,128)}, f32[2,64,128,128]{3,2,1,0:T(8,128)S(1)}, u32[]{:S(2)}) copy-start(f32[2,64,128,128]{3,2,1,0:T(8,128)S(1)} %fusion.8) | copy-start | bytes 25165828
  182.3 22.2 %slice-start = ((s8[8388608]{0:T(1024)(128)(4,1)}), s8[4194304]{0:T(1024)(128)(4,1)S(1)}, s32[]{:S(2)}) async-start(s8[8388608]{0:T(1024)(128)(4,1)} %bitcast.235), calls=%async_computation.4 | async-start | bytes 8388608
  191.1 13.4 %slice-start.1 = ((s8[8388608]{0:T(1024)(128)(4,1)}), s8[4194304]{0:T(1024)(128)(4,1)S(1)}, s32[]{:S(2)}) async-start(s8[8388608]{0:T(1024)(128)(4,1)} %bitcast.235), calls=%async_computation.5 | async-start | bytes 8388608
  268.7 31.1 %copy-start.11 = (pred[2,4]{1,0:T(4,128)(4,1)S(1)}, pred[2,4]{1,0:T(4,128)(4,1)}, u32[]{:S(2)}) copy-start(pred[2,4]{1,0:T(4,128)(4,1)} %broadcast_in_dim.31) | copy-start | bytes 28
  278.5 45.8 %copy-start.6 = (f32[32,64]{1,0:T(8,128)S(1)}, f32[32,64]{1,0:T(8,128)}, u32[]{:S(2)}) copy-start(f32[32,64]{1,0:T(8,128)} %get-tuple-element.92) | copy-start | bytes 24580
  278.5 45.8 %copy-start.7 = (f32[32,64]{1,0:T(8,128)S(1)}, f32[32,64]{1,0:T(8,128)}, u32[]{:S(2)}) copy-start(f32[32,64]{1,0:T(8,128)} %get-tuple-element.93) | copy-start | bytes 24580
  300.7 23.1 %all-to-all-start.2 = ((bf16[8,16,256]{2,1,0:T(8,128)(2,1)}), bf16[8,16,256]{2,1,0:T(8,128)(2,1)S(1)}, u32[]{:S(2)}, u32[]{:S(2)}) async-start(bf16[8,16,256]{2,1,0:T(8,128)(2,1)} %convert_element_type.425), calls=%async_computation.2 | async-start | bytes 131072 | tf_op jit(solution)/shard_map/all_to_all | solution.py:231
  329.1 16.6 %all-to-all-start.3 = ((bf16[128,2,256]{2,1,0:T(2,128)(2,1)}), bf16[128,2,256]{2,1,0:T(2,128)(2,1)S(1)}, u32[]{:S(2)}, u32[]{:S(2)}) async-start(bf16[128,2,256]{2,1,0:T(2,128)(2,1)} %reshape.531), calls=%async_computation.3 | async-start | bytes 262144 | tf_op jit(solution)/shard_map/all_to_all | solution.py:241
  (2 other events, 9.7 us)
